TPU v7x, 32 devices: a whole 2x2x4 slice. The times are simulated.
32 devices in a mesh: space: 8 (over z, x), tm: 4 (over y, core).
Axes of the slice: x: 2, y: 2, z: 4, core: 2. Of those that a mesh axis runs over, the one named last changes fastest.
Arguments:
- latents: bfloat16 [4, 16, 120, 384], P('tm', 'space'), may hold values from -6 to 6
- conv_gain: float32 [384], replicated, may hold values from 0.25 to 1.75
- conv_weight: bfloat16 [3, 3, 3, 384, 384], replicated, may hold values from -0.0625 to 0.0625
- conv_bias: float32 [384], replicated, may hold values from -3 to 3
- attn_gain: float32 [384], replicated, may hold values from 0.25 to 1.75
- qkv_weight: bfloat16 [384, 1152], replicated, may hold values from -2 to 2, as said below
- proj_weight: bfloat16 [384, 384], replicated, may hold values from -0.3125 to 0.3125
- proj_bias: float32 [384], replicated, may hold values from -3 to 3
Outputs:
- decoded: float32 [4, 16, 120, 384], P('tm', 'space')
Inputs may be any that keep to these rules, and one draw needn't show every extreme that they name: qkv_weight is real-valued with independent entries.
All inputs are finite; a program needn't handle non-finite values.
Results may differ from a plain program's by a relative error of at most 0.0095.
The roundings to bfloat16 on the way count: a program that leaves them out, or rounds other values in their place, can miss the bound.
Values may be sent and summed in bfloat16 or wider, within the bound.
A program may use at most 128 MiB of HBM per device.

v0:
```python
import jax
import jax.numpy as jnp
from jax import lax
from jax.sharding import PartitionSpec as P


def passed_along(value, axis, steps):
    count = lax.axis_size(axis)
    leading, last = (max(0, -steps), min(count, count - steps))
    return lax.ppermute(value, axis, [(source, source + steps) for source in range(leading, last)])


def extended(cells, sides, width):
    for axis, dim in sides:
        count = lax.axis_size(axis)
        ends = count - 1
        head = lax.slice_in_dim(cells, 0, width, axis=dim)
        tail = lax.slice_in_dim(cells, cells.shape[dim] - width, cells.shape[dim], axis=dim)
        cells = jnp.concatenate(
            [
                lax.ppermute(tail, axis, [(i, (i + 1) % count) for i in range(ends)]),
                cells,
                lax.ppermute(head, axis, [((i + 1) % count, i) for i in range(ends)]),
            ],
            axis=dim,
        )
    return cells


def normed(v, gain):
    v = v.astype(jnp.float32)
    return v * lax.rsqrt(jnp.mean(v * v, axis=-1, keepdims=True) + 1e-06) * gain


def frame_context(act):
    earlier = passed_along(act, "tm", 1)
    oldest = passed_along(act, "tm", 2)
    stacked = jnp.concatenate([oldest, earlier, act], axis=0)
    rimmed = extended(stacked, (("space", 1),), 1)
    return jnp.pad(rimmed, ((0, 0), (0, 0), (1, 1), (0, 0)))


def causal_conv(act, weight, bias):
    rows, cols, chans = (act.shape[1], act.shape[2], act.shape[3])
    outputs = weight.shape[4]
    rimmed = frame_context(act)
    running = jnp.zeros((rows * cols, outputs), jnp.float32)
    for i in range(3):
        for j in range(3):
            for k in range(3):
                window = rimmed[i, j : j + rows, k : k + cols, :].reshape(rows * cols, chans)
                running = running + jnp.dot(
                    window, weight[i, j, k], preferred_element_type=jnp.float32
                )
    return (running + bias).reshape(1, rows, cols, outputs)


def softmax_update(carry, queries, keys, values, scale):
    highest, denom, accum = carry
    scores = jnp.dot(queries, keys.T, preferred_element_type=jnp.float32) * scale
    new_high = jnp.max(scores, axis=-1)
    factor = jnp.exp(highest - new_high)
    weights = jnp.exp(scores - new_high[:, None])
    denom = denom * factor + jnp.sum(weights, axis=-1)
    accum = accum * factor[:, None] + jnp.dot(
        weights.astype(jnp.bfloat16), values, preferred_element_type=jnp.float32
    )
    return (new_high, denom, accum)


def on_device(
    latents, conv_gain, conv_weight, conv_bias, attn_gain, qkv_weight, proj_weight, proj_bias
):
    conv_act = jax.nn.silu(normed(latents, conv_gain)).astype(jnp.bfloat16)
    block_out = latents.astype(jnp.float32) + causal_conv(conv_act, conv_weight, conv_bias)
    frames, rows, cols, chans = block_out.shape
    attn_in = normed(block_out, attn_gain).astype(jnp.bfloat16).reshape(rows * cols, chans)
    queries = jnp.dot(attn_in, qkv_weight[:, :chans], preferred_element_type=jnp.float32).astype(
        jnp.bfloat16
    )
    scale = chans ** (-0.5)
    initial = (
        jnp.full((rows * cols,), -jnp.inf, jnp.float32),
        jnp.zeros((rows * cols,), jnp.float32),
        jnp.zeros((rows * cols, chans), jnp.float32),
    )
    keys = jnp.dot(
        attn_in, qkv_weight[:, chans : 2 * chans], preferred_element_type=jnp.float32
    ).astype(jnp.bfloat16)
    values = jnp.dot(
        attn_in, qkv_weight[:, 2 * chans :], preferred_element_type=jnp.float32
    ).astype(jnp.bfloat16)
    final = softmax_update(
        initial,
        queries,
        lax.all_gather(keys, "space", axis=0, tiled=True),
        lax.all_gather(values, "space", axis=0, tiled=True),
        scale,
    )
    mixed = (final[2] / final[1][:, None]).astype(jnp.bfloat16)
    projected = jnp.dot(mixed, proj_weight, preferred_element_type=jnp.float32) + proj_bias
    decoded = block_out.reshape(rows * cols, chans) + projected
    return decoded.reshape(frames, rows, cols, chans)


def solution(mesh):
    in_specs = (P("tm", "space", None, None), P(), P(), P(), P(), P(), P(), P())
    out_specs = P("tm", "space", None, None)
    return jax.shard_map(
        on_device, mesh=mesh, in_specs=in_specs, out_specs=out_specs, check_vma=False
    )
```

profile of v0, /device:TPU:4, one launch (start us, length us, event | category | flops | bytes accessed | tf_op | source)
XLA Modules:
  0.0 143.4 jit_solution(7200497221690679485)
XLA Ops:
  6.5 1.2 fusion.23
  7.7 1.4 fusion.30
  9.1 1.3 collective-permute-start
  10.4 1.9 %collective-permute-start.1 = (bf16[1,2,120,384]{3,2,1,0:T(8,128)(2,1)S(1)}, bf16[1,2,120,384]{3,2,1,0:T(8,128)(2,1)S(1)}, u32[]{:S(2)}, u32[]{:S(2)}) collective-permute-start(bf16[1,2,120,384]{3,2,1,0:T(8,128)(2,1)S(1)} %fusion.30), channel_id=1, source_target_pairs={{0,1},{1,2},{2,3},{4,5},{5,6},{6,7},{8,9},{9,10},{10,11},{12,13},{... | collective-permute-start | bytes 552968 | tf_op jit(solution)/shard_map/ppermute | solution.py:10
  12.4 6.2 %collective-permute-done = bf16[1,2,120,384]{3,2,1,0:T(8,128)(2,1)S(1)} collective-permute-done((bf16[1,2,120,384]{3,2,1,0:T(8,128)(2,1)S(1)}, bf16[1,2,120,384]{3,2,1,0:T(8,128)(2,1)S(1)}, u32[]{:S(2)}, u32[]{:S(2)}) %collective-permute-start) | collective-permute-done | bytes 184352 | tf_op jit(solution)/shard_map/ppermute | solution.py:10
  18.6 0.8 collective-permute-done.1
  19.5 3.4 %collective-permute-start.2 = (bf16[3,1,120,384]{3,2,1,0:T(8,128)(2,1)S(1)}, bf16[3,1,120,384]{3,2,1,0:T(8,128)(2,1)S(1)}, u32[]{:S(2)}, u32[]{:S(2)}) collective-permute-start(bf16[3,1,120,384]{3,2,1,0:T(8,128)(2,1)S(1)} %get-tuple-element.31), channel_id=1, source_target_pairs={{0,4},{4,8},{8,12},{12,16},{16,20},{20,24},{24,28},{1,5},{5,9},{9,... | collective-permute-start | bytes 829448 | tf_op jit(solution)/shard_map/ppermute | solution.py:21
  23.0 1.3 collective-permute-start.3
  24.3 8.6 %collective-permute-done.2 = bf16[3,1,120,384]{3,2,1,0:T(8,128)(2,1)S(1)} collective-permute-done((bf16[3,1,120,384]{3,2,1,0:T(8,128)(2,1)S(1)}, bf16[3,1,120,384]{3,2,1,0:T(8,128)(2,1)S(1)}, u32[]{:S(2)}, u32[]{:S(2)}) %collective-permute-start.2) | collective-permute-done | bytes 276512 | tf_op jit(solution)/shard_map/ppermute | solution.py:21
  32.9 0.4 select_maximum_fusion
  33.3 0.5 fusion.100
  33.8 0.3 fusion.64
  34.1 0.3 fusion.58
  34.4 0.3 fusion.54
  34.7 0.3 fusion.50
  35.0 0.3 fusion.46
  35.3 0.3 fusion.42
  35.5 0.3 fusion.38
  35.8 0.3 fusion.31
  36.1 0.1 pad_maximum_fusion.4
  36.2 0.3 convolution_add_fusion.20
  36.5 0.3 convolution_add_fusion.19
  36.8 0.3 convolution_add_fusion.18
  37.1 0.3 fusion.3
  37.4 0.3 convolution_add_fusion.16
  37.8 0.3 fusion.4
  38.1 0.3 convolution_add_fusion.14
  38.4 0.3 fusion.5
  38.7 0.3 convolution_add_fusion.12
  39.0 0.3 fusion.6
  39.3 0.3 convolution_add_fusion.10
  39.6 0.3 fusion.7
  39.9 0.3 convolution_add_fusion.8
  40.2 0.3 fusion.8
  40.5 0.3 convolution_add_fusion.6
  40.8 0.3 convolution_add_fusion.5
  41.1 0.3 convolution_add_fusion.4
  41.4 0.3 convolution_add_fusion.3
  41.7 0.3 fusion.10
  42.0 0.1 multiply_reduce_fusion
  42.2 0.1 multiply_convert_fusion
  42.3 1.0 convolution_convert_fusion.1
  43.3 1.0 convolution_convert_fusion
  44.3 45.1 %all-gather.3.cloned.1.call-done = bf16[1920,384]{1,0:T(8,128)(2,1)} async-done(((bf16[240,384]{1,0:T(8,128)(2,1)}), bf16[1920,384]{1,0:T(8,128)(2,1)}) %all-gather.3.cloned.1.call-update) | async-done | bytes 1474576 | tf_op jit(solution)/shard_map/all_gather | solution.py:96
  89.4 2.5 %fusion.102 = (f32[240]{0:T(256)S(1)}, f32[240,1920]{1,0:T(8,128)S(1)}) fusion(bf16[1920,384]{1,0:T(8,128)(2,1)} %all-gather.3.cloned.1.call-done, bf16[240,384]{1,0:T(8,128)(2,1)S(1)} %bitcast.150, bf16[384,1152]{1,0:T(8,128)(2,1)} %param.13), kind=kOutput, calls=%fused_computation.147 | convolution fusion | flops 425686784 | bytes 3797952 | tf_op jit(solution)/shard_map/dot_general | solution.py:60
  91.8 0.4 fusion.1
  92.2 41.2 %all-gather.5.cloned.1.call-done = bf16[1920,384]{1,0:T(8,128)(2,1)} async-done(((bf16[240,384]{1,0:T(8,128)(2,1)}), bf16[1920,384]{1,0:T(8,128)(2,1)}) %all-gather.5.cloned.1.call-update) | async-done | bytes 1474576 | tf_op jit(solution)/shard_map/all_gather | solution.py:97
  133.5 3.1 %fusion.12 = f32[240,384]{1,0:T(8,128)} fusion(f32[240,384]{1,0:T(8,128)S(1)} %bitcast.151, bf16[384,384]{1,0:T(8,128)(2,1)S(1)} %copy-done, bf16[1920,384]{1,0:T(8,128)(2,1)} %all-gather.5.cloned.1.call-done, f32[240,1920]{1,0:T(8,128)S(1)} %get-tuple-element.36, f32[240]{0:T(256)S(1)} %get-tuple-element.35, f32[384]{0:T(512)S(1)} %copy-done.6, ...), kind=kOutput, calls=%fused_computation.37 | convolution fusion | flops 426055680 | bytes 4354368 | tf_op jit(solution)/shard_map/dot_general | solution.py:101
  (25 shorter events, 0.4 us)
Async XLA Ops:
  6.5 127.0 %copy-start = (bf16[384,384]{1,0:T(8,128)(2,1)S(1)}, bf16[384,384]{1,0:T(8,128)(2,1)}, u32[]{:S(2)}) copy-start(bf16[384,384]{1,0:T(8,128)(2,1)} %param.14) | copy-start | bytes 884740
  6.5 82.8 %all-gather.3.cloned.1.call-start = ((), (), s32[]{:S(2)}) async-start(), calls=%async_computation | async-start | bytes 1658880 | tf_op jit(solution)/shard_map/all_gather | solution.py:96
  6.5 27.3 %copy-start.1 = (bf16[3,3,3,384,384]{4,3,2,1,0:T(8,128)(2,1)S(1)}, bf16[3,3,3,384,384]{4,3,2,1,0:T(8,128)(2,1)}, u32[]{:S(2)}) copy-start(bf16[3,3,3,384,384]{4,3,2,1,0:T(8,128)(2,1)} %param.10) | copy-start | bytes 23887876
  9.1 9.4 %collective-permute-start = (bf16[1,2,120,384]{3,2,1,0:T(8,128)(2,1)S(1)}, bf16[1,2,120,384]{3,2,1,0:T(8,128)(2,1)S(1)}, u32[]{:S(2)}, u32[]{:S(2)}) collective-permute-start(bf16[1,2,120,384]{3,2,1,0:T(8,128)(2,1)S(1)} %fusion.30), channel_id=1, source_target_pairs={{0,2},{1,3},{4,6},{5,7},{8,10},{9,11},{12,14},{13,15},{16,18},{17,... | collective-permute-start | bytes 552968 | tf_op jit(solution)/shard_map/ppermute | solution.py:10
  10.4 8.9 %collective-permute-start.1 = (bf16[1,2,120,384]{3,2,1,0:T(8,128)(2,1)S(1)}, bf16[1,2,120,384]{3,2,1,0:T(8,128)(2,1)S(1)}, u32[]{:S(2)}, u32[]{:S(2)}) collective-permute-start(bf16[1,2,120,384]{3,2,1,0:T(8,128)(2,1)S(1)} %fusion.30), channel_id=1, source_target_pairs={{0,1},{1,2},{2,3},{4,5},{5,6},{6,7},{8,9},{9,10},{10,11},{12,13},{... | collective-permute-start | bytes 552968 | tf_op jit(solution)/shard_map/ppermute | solution.py:10
  19.5 13.4 %collective-permute-start.2 = (bf16[3,1,120,384]{3,2,1,0:T(8,128)(2,1)S(1)}, bf16[3,1,120,384]{3,2,1,0:T(8,128)(2,1)S(1)}, u32[]{:S(2)}, u32[]{:S(2)}) collective-permute-start(bf16[3,1,120,384]{3,2,1,0:T(8,128)(2,1)S(1)} %get-tuple-element.31), channel_id=1, source_target_pairs={{0,4},{4,8},{8,12},{12,16},{16,20},{20,24},{24,28},{1,5},{5,9},{9,... | collective-permute-start | bytes 829448 | tf_op jit(solution)/shard_map/ppermute | solution.py:21
  23.0 9.9 %collective-permute-start.3 = (bf16[3,1,120,384]{3,2,1,0:T(8,128)(2,1)S(1)}, bf16[3,1,120,384]{3,2,1,0:T(8,128)(2,1)S(1)}, u32[]{:S(2)}, u32[]{:S(2)}) collective-permute-start(bf16[3,1,120,384]{3,2,1,0:T(8,128)(2,1)S(1)} %get-tuple-element.32), channel_id=1, source_target_pairs={{4,0},{8,4},{12,8},{16,12},{20,16},{24,20},{28,24},{5,1},{9,5},{13... | collective-permute-start | bytes 829448 | tf_op jit(solution)/shard_map/ppermute | solution.py:23
  38.1 3.6 %copy-start.4 = (f32[384]{0:T(512)S(1)}, f32[384]{0:T(512)}, u32[]{:S(2)}) copy-start(f32[384]{0:T(512)} %param.11) | copy-start | bytes 4612
  38.4 3.6 %copy-start.2 = (bf16[1,2,120,384]{3,2,1,0:T(8,128)(2,1)S(1)}, bf16[1,2,120,384]{3,2,1,0:T(8,128)(2,1)}, u32[]{:S(2)}) copy-start(bf16[1,2,120,384]{3,2,1,0:T(8,128)(2,1)} %param.8) | copy-start | bytes 552964
  38.7 3.5 %copy-start.5 = (f32[384]{0:T(512)S(1)}, f32[384]{0:T(512)}, u32[]{:S(2)}) copy-start(f32[384]{0:T(512)} %param.12) | copy-start | bytes 4612
  38.7 3.6 %copy-start.3 = (bf16[384,1152]{1,0:T(8,128)(2,1)S(1)}, bf16[384,1152]{1,0:T(8,128)(2,1)}, u32[]{:S(2)}) copy-start(bf16[384,1152]{1,0:T(8,128)(2,1)} %param.13) | copy-start | bytes 2654212
  40.5 93.0 %copy-start.6 = (f32[384]{0:T(512)S(1)}, f32[384]{0:T(512)}, u32[]{:S(2)}) copy-start(f32[384]{0:T(512)} %param.15) | copy-start | bytes 4612
  43.3 90.2 %all-gather.5.cloned.1.call-start = ((), (), s32[]{:S(2)}) async-start(), calls=%async_computation.1 | async-start | bytes 1658880 | tf_op jit(solution)/shard_map/all_gather | solution.py:97
Sparse Core Ops, SparseCore 0:
  43.4 45.9 all-gather.2
  91.5 41.9 all-gather.4
where the time goes:
time: 145 us; the launch traced here: 143 us
  waiting for transfers between devices  102 us (70%)
  matrix products  15.2 us (10%)
  between operations  13.7 us (9%)
  starting transfers between devices  7.96 us (5%)
  other arithmetic  3.87 us (3%)
    all_gather x1, waiting for transfers between devices, on_device(): lax.all_gather(keys, 'space', axis=0, tiled=True)  45.1 us
    all_gather x1, waiting for transfers between devices, on_device(): lax.all_gather(values, 'space', axis=0, tiled=True)  41.2 us
    ppermute x1, waiting for transfers between devices, extended(): lax.ppermute(tail, axis, [(i, (i + 1) % count) for i in range(ends)])  8.63 us
    dot_general x27, matrix products, causal_conv(): jnp.dot(window, weight[i, j, k], preferred_element_type=jnp.float32)  7.76 us
    ppermute x2, waiting for transfers between devices, passed_along(): lax.ppermute(value, axis, [(source, source + steps) for source in range(l...  7.02 us
    ppermute x1, starting transfers between devices, extended(): lax.ppermute(tail, axis, [(i, (i + 1) % count) for i in range(ends)])  3.41 us
    ppermute x2, starting transfers between devices, passed_along(): lax.ppermute(value, axis, [(source, source + steps) for source in range(l...  3.21 us
    dot_general x1, matrix products, on_device(): jnp.dot(mixed, proj_weight, preferred_element_type=jnp.float32) + proj_bias  3.07 us
  transfers between devices with their start and end apart: 6, of which 5 were waited for; matrix products, arithmetic and copies ran while one was open for 3% of the time, Pallas kernels for 0%

commit v1 on v0

v1 whole, which is shorter than its diff:
```python
import functools

import jax
import jax.numpy as jnp
from jax import lax
from jax.experimental import pallas as pl
from jax.experimental.pallas import tpu as pltpu
from jax.sharding import PartitionSpec as P

MESH = pl.DeviceIdType.MESH
F32, BF16 = jnp.float32, jnp.bfloat16


def normed(v, gain):
    return v * lax.rsqrt(jnp.mean(v * v, axis=-1, keepdims=True) + 1e-06) * gain


def dot(a, b):
    return jnp.dot(a, b, preferred_element_type=F32)


def kernel(
    count, frames, padded,
    lat_hbm, cgain, cw_hbm, cbias, again, qkv_hbm, proj_hbm, pbias, out,
    lat, cw, qkv, proj, frame, taps, block, gathered, query, high, denom, accum,
    in_sem, cw_sem, send, recv, up1, dn1, up2, dn2, to_a, to_b, line_sem, b_sem, a_sem, b_dn_sem,
):
    t, s = lax.axis_index("tm"), lax.axis_index("space")
    rows, cols, chans = lat.shape[1:]
    cells = rows * cols
    na = cells - (cells * 2 // 5) // 16 * 16
    nb = cells - na
    hi, lo = lax.div(s, 2), lax.rem(s, 2)
    nhi = count // 2
    mate = s + 1 - 2 * lo
    twin = t + 1 - 2 * lax.rem(t, 2)
    has_up, has_dn = s > 0, s < count - 1
    old = t >= 2
    near = [
        (s >= 1, {"space": s - 1}),
        (s < count - 1, {"space": s + 1}),
        (s >= 2, {"space": s - 2}),
        (s < count - 2, {"space": s + 2}),
        (t >= 2, {"tm": t - 2}),
        (t < frames - 2, {"tm": t + 2}),
        (True, {"tm": twin}),
    ]
    barrier = pltpu.get_barrier_semaphore()
    for there, device in near:
        @pl.when(there)
        def _():
            pl.semaphore_signal(barrier, inc=1, device_id=device, device_id_type=MESH)

    get_lat = pltpu.make_async_copy(lat_hbm, lat, in_sem.at[0])
    get_qkv = pltpu.make_async_copy(qkv_hbm, qkv, in_sem.at[1])
    get_proj = pltpu.make_async_copy(proj_hbm, proj, in_sem.at[2])
    get_cw = [pltpu.make_async_copy(cw_hbm.at[i], cw.at[i], cw_sem.at[i]) for i in range(3)]
    get_lat.start()
    for i in (2, 0, 1):
        get_cw[i].start()
    get_qkv.start()
    get_proj.start()

    def zero_row(f, r):
        frame[f, r] = jnp.zeros((padded, chans), BF16)

    @pl.when(s == 0)
    def _():
        zero_row(2, 0)
        zero_row(0, 0)

    @pl.when(s == count - 1)
    def _():
        zero_row(2, rows + 1)
        zero_row(0, rows + 1)

    get_lat.wait()
    for r in range(rows):
        act = jax.nn.silu(normed(lat[0, r].astype(F32), cgain[...]))
        act = jnp.concatenate([act, jnp.zeros((padded - cols, chans), F32)], axis=0)
        frame[2, r + 1] = act.astype(BF16)

    pl.semaphore_wait(barrier, sum(there.astype(jnp.int32) for there, _ in near[:-1]) + 1)

    def remote(src, dst, ssem, rsem, device):
        return pltpu.make_async_remote_copy(
            src_ref=src, dst_ref=dst, send_sem=ssem, recv_sem=rsem,
            device_id=device, device_id_type=MESH,
        )

    body = pl.ds(1, rows)
    later = remote(frame.at[2, body], frame.at[0, body], send.at[0], recv.at[0], {"tm": t + 2})
    own_up = remote(frame.at[2, 1], frame.at[2, rows + 1], send.at[1], recv.at[1], {"space": s - 1})
    own_dn = remote(frame.at[2, rows], frame.at[2, 0], send.at[2], recv.at[2], {"space": s + 1})
    old_up = remote(frame.at[0, 1], frame.at[0, rows + 1], send.at[3], recv.at[3], {"space": s - 1})
    old_dn = remote(frame.at[0, rows], frame.at[0, 0], send.at[4], recv.at[4], {"space": s + 1})
    twin_own = remote(frame.at[2], frame.at[1], send.at[5], recv.at[5], {"tm": twin})
    twin_old = remote(frame.at[0], frame.at[1], send.at[5], recv.at[5], {"tm": twin})
    is_even = lax.rem(t, 2) == 0
    gives_old = jnp.logical_and(t >= 3, jnp.logical_not(is_even))

    pl.when(t < frames - 2)(later.start)
    pl.when(has_up)(own_up.start)
    pl.when(has_dn)(own_dn.start)

    @pl.when(old)
    def _():
        later.wait_recv()
        pl.when(has_up)(old_up.start)
        pl.when(has_dn)(old_dn.start)

    pl.when(has_dn)(own_up.wait_recv)
    pl.when(has_up)(own_dn.wait_recv)
    pl.when(is_even)(twin_own.start)

    def conv_step(i, first):
        left = jnp.concatenate(
            [frame[i, pl.ds(j, rows)].reshape(rows * padded, chans) for j in range(3)], axis=1
        )
        for k in range(3):
            right = jnp.concatenate([cw[i, j, k] for j in range(3)], axis=0)
            part = dot(left, right)
            taps[k] = part if first else taps[k] + part

    get_cw[2].wait()
    conv_step(2, True)
    get_cw[0].wait()

    @pl.when(old)
    def _():
        pl.when(has_dn)(old_up.wait_recv)
        pl.when(has_up)(old_dn.wait_recv)
        pl.when(gives_old)(twin_old.start)
        conv_step(0, False)

    get_cw[1].wait()

    @pl.when(t >= 1)
    def _():
        twin_own.wait_recv()
        conv_step(1, False)

    for r in range(rows):
        at = pl.ds(r * padded, padded)
        sums = pltpu.roll(taps[0, at], 1, 0) + taps[1, at] + pltpu.roll(taps[2, at], padded - 1, 0)
        sums = sums[:cols] + cbias[...]
        block[pl.ds(r * cols, cols)] = lat[0, r].astype(F32) + sums
    attn_in = normed(block[...], again[...]).astype(BF16)
    gathered[s] = attn_in

    part_a, part_b = pl.ds(0, na), pl.ds(na, nb)

    def line(sems, rsems, h, lane, step, part=None):
        ref = gathered.at[2 * h + lane]
        ref = ref if part is None else gathered.at[2 * h + lane, part]
        return remote(ref, ref, sems.at[h], rsems.at[h], {"space": s + 2 * step})

    def full_up(h):
        return line(up1, line_sem, h, lo, 1)

    def full_dn(h):
        return line(dn1, line_sem, h, lo, -1)

    def b_up(h):
        return line(up2, b_sem, h, 1 - lo, 1, part_b)

    def b_dn(h):
        return line(dn2, b_sem, h, 1 - lo, -1, part_b)

    def a_over(h, mine):
        ref = gathered.at[2 * h + jnp.where(mine, lo, 1 - lo), part_a]
        return remote(ref, ref, to_a.at[h], a_sem.at[h], {"space": mate})

    def b_over(mine):
        ref = gathered.at[2 * hi + jnp.where(mine, lo, 1 - lo), part_b]
        return remote(ref, ref, to_b.at[0], b_dn_sem.at[0], {"space": mate})

    above, below = hi < nhi - 1, hi > 0
    b_over(True).start()
    pl.when(above)(full_up(hi).start)
    pl.when(below)(full_dn(hi).start)
    a_over(hi, True).start()

    get_qkv.wait()
    get_proj.wait()
    query[...] = dot(attn_in, qkv[:, :chans]).astype(BF16)
    high[...] = jnp.full(high.shape, -jnp.inf, F32)
    denom[...] = jnp.zeros(denom.shape, F32)
    accum[...] = jnp.zeros(accum.shape, F32)

    b_over(False).wait_recv()
    pl.when(above)(b_up(hi).start)
    pl.when(below)(b_dn(hi).start)
    a_over(hi, False).wait_recv()

    def attend(h):
        feats = gathered[pl.ds(2 * h, 2)].reshape(2 * cells, chans)
        keys = dot(feats, qkv[:, chans : 2 * chans]).astype(BF16)
        values = dot(feats, qkv[:, 2 * chans :]).astype(BF16)
        scores = lax.dot_general(
            query[...], keys, (((1,), (1,)), ((), ())), preferred_element_type=F32
        ) * (chans ** -0.5)
        top = jnp.maximum(high[...], jnp.max(scores, axis=-1, keepdims=True))
        factor = jnp.exp(high[...] - top)
        weights = jnp.exp(scores - top)
        high[...] = top
        denom[...] = denom[...] * factor + jnp.sum(weights, axis=-1, keepdims=True)
        accum[...] = accum[...] * factor + dot(weights.astype(BF16), values)

    attend(hi)

    def arrive(h, here, onward, first, second):
        @pl.when(here)
        def _():
            first(h).wait_recv()
            pl.when(onward)(first(h).start)
            a_over(h, True).start()

    def arrive_b(h, here, onward, second):
        @pl.when(here)
        def _():
            second(h).wait_recv()
            pl.when(onward)(second(h).start)

    def finish(h, here):
        @pl.when(here)
        def _():
            a_over(h, False).wait_recv()
            attend(h)

    def step(d, carry):
        from_below, from_above = hi - d, hi + d
        low_here, up_here = from_below >= 0, from_above < nhi
        arrive(from_below, low_here, above, full_up, b_up)
        arrive(from_above, up_here, below, full_dn, b_dn)
        arrive_b(from_below, low_here, above, b_up)
        arrive_b(from_above, up_here, below, b_dn)
        finish(from_below, low_here)
        finish(from_above, up_here)
        return carry

    lax.fori_loop(1, nhi, step, 0)

    mixed = (accum[...] / denom[...]).astype(BF16)
    decoded = block[...] + (dot(mixed, proj[...]) + pbias[...])
    for r in range(rows):
        out[0, r] = decoded[r * cols : (r + 1) * cols]

    pl.when(t < frames - 2)(later.wait_send)
    pl.when(has_up)(own_up.wait_send)
    pl.when(has_dn)(own_dn.wait_send)
    pl.when(jnp.logical_and(old, has_up))(old_up.wait_send)
    pl.when(jnp.logical_and(old, has_dn))(old_dn.wait_send)
    pl.when(is_even)(twin_own.wait_send)
    pl.when(gives_old)(twin_old.wait_send)
    b_over(True).wait_send()

    def drain(h, carry):
        a_over(h, True).wait_send()

        @pl.when(jnp.logical_and(h <= hi, above))
        def _():
            full_up(h).wait_send()
            b_up(h).wait_send()

        @pl.when(jnp.logical_and(h >= hi, below))
        def _():
            full_dn(h).wait_send()
            b_dn(h).wait_send()

        return carry

    lax.fori_loop(0, nhi, drain, 0)


def solution(mesh):
    count, frames = mesh.shape["space"], mesh.shape["tm"]

    def on_device(
        latents, conv_gain, conv_weight, conv_bias, attn_gain, qkv_weight, proj_weight, proj_bias
    ):
        _, rows, cols, chans = latents.shape
        padded = (cols + 16) // 16 * 16
        cells = rows * cols
        nhi = count // 2
        anywhere = pl.BlockSpec(memory_space=pl.ANY)
        local = pl.BlockSpec(memory_space=pltpu.VMEM)
        dma = pltpu.SemaphoreType.DMA
        return pl.pallas_call(
            functools.partial(kernel, count, frames, padded),
            out_shape=jax.ShapeDtypeStruct(latents.shape, F32),
            in_specs=[anywhere, local, anywhere, local, local, anywhere, anywhere, local],
            out_specs=local,
            scratch_shapes=[
                pltpu.VMEM(latents.shape, BF16),
                pltpu.VMEM(conv_weight.shape, BF16),
                pltpu.VMEM(qkv_weight.shape, BF16),
                pltpu.VMEM(proj_weight.shape, BF16),
                pltpu.VMEM((3, rows + 2, padded, chans), BF16),
                pltpu.VMEM((3, rows * padded, chans), F32),
                pltpu.VMEM((cells, chans), F32),
                pltpu.VMEM((count, cells, chans), BF16),
                pltpu.VMEM((cells, chans), BF16),
                pltpu.VMEM((cells, 1), F32),
                pltpu.VMEM((cells, 1), F32),
                pltpu.VMEM((cells, chans), F32),
                dma((3,)), dma((3,)), dma((6,)), dma((6,)),
                dma((nhi,)), dma((nhi,)), dma((nhi,)), dma((nhi,)), dma((nhi,)), dma((1,)),
                dma((nhi,)), dma((nhi,)), dma((nhi,)), dma((1,)),
            ],
            compiler_params=pltpu.CompilerParams(
                collective_id=0, has_side_effects=True, vmem_limit_bytes=48 * 2**20
            ),
        )(
            latents, conv_gain.reshape(1, chans), conv_weight, conv_bias.reshape(1, chans),
            attn_gain.reshape(1, chans), qkv_weight, proj_weight, proj_bias.reshape(1, chans),
        )

    in_specs = (P("tm", "space", None, None), P(), P(), P(), P(), P(), P(), P())
    return jax.shard_map(
        on_device, mesh=mesh, in_specs=in_specs,
        out_specs=P("tm", "space", None, None), check_vma=False,
    )
```

time: 145 us -> 45.3 us (0.31)
  waiting for transfers between devices: 102 us -> 0 us
  Pallas kernels: 0 us -> 38.5 us
  matrix products: 15.2 us -> 0 us
  between operations: 13.7 us -> 0.01 us
  starting transfers between devices: 7.96 us -> 0 us
  local copies, waits for them, and re-layouts: 0.62 us -> 6.52 us
  other arithmetic: 3.87 us -> 0 us
    all_gather x2 -> x0, waiting for transfers between devices: 86.3 us -> none  [the longest x1 45.1 us: on_device(): lax.all_gather(keys, 'space', axis=0, tiled=True)]
    pallas_call x0 -> x1, Pallas kernels: none -> 38.5 us  [on_device(): pl.pallas_call(functools.partial(kernel, count, frames, padded), out_shap...]
    ppermute x4 -> x0, waiting for transfers between devices: 15.7 us -> none  [the longest x1 8.63 us: extended(): lax.ppermute(tail, axis, [(i, (i + 1) % count) for i in range(ends)])]
    dot_general x31 -> x0, matrix products: 15.2 us -> none  [the longest x27 7.76 us: causal_conv(): jnp.dot(window, weight[i, j, k], preferred_element_type=jnp.float32)]
    ppermute x4 -> x0, starting transfers between devices: 7.92 us -> none  [the longest x1 3.41 us: extended(): lax.ppermute(tail, axis, [(i, (i + 1) % count) for i in range(ends)])]
    unnamed x14 -> x7, local copies, waits for them, and re-layouts: 0.04 us -> 3.79 us
    reshape x0 -> x4, local copies, waits for them, and re-layouts: none -> 2.73 us  [the longest x1 0.68 us: on_device(): conv_bias.reshape(1, chans)]
    reduce_sum x3 -> x0, other arithmetic: 1.73 us -> none  [the longest x2 1.33 us: normed(): return v * lax.rsqrt(jnp.mean(v * v, axis=-1, keepdims=True) + 1e-06) * gain]
  transfers between devices with their start and end apart: 6 -> 0, of which waited for: 5 -> 0; matrix products, arithmetic and copies ran while one was open for 3% -> 0% of each run, Pallas kernels for 0% -> 0%
where the time goes in v1:
time: 45.3 us; the launch traced here: 45 us
  Pallas kernels  38.5 us (85%)
  local copies, waits for them, and re-layouts  6.52 us (14%)
    pallas_call x1, Pallas kernels, on_device(): pl.pallas_call(functools.partial(kernel, count, frames, padded), out_shap...  38.5 us
    unnamed x7, local copies, waits for them, and re-layouts  3.79 us

profile of v1, /device:TPU:4, one launch (start us, length us, event | category | flops | bytes accessed | tf_op | source)
XLA Modules:
  0.0 45.0 jit_solution(1258567303266623911)
XLA Ops:
  0.0 0.7 %reshape.12.cgain = f32[1,384]{1,0:T(1,128)S(1)} reshape(f32[384]{0:T(512)} %param.9) | data formatting | bytes 3072 | tf_op jit(solution)/shard_map/reshape | solution.py:315
  0.7 0.7 %reshape.13.cbias = f32[1,384]{1,0:T(1,128)S(1)} reshape(f32[384]{0:T(512)} %param.11) | data formatting | bytes 3072 | tf_op jit(solution)/shard_map/reshape | solution.py:315
  1.4 0.7 %reshape.14.again = f32[1,384]{1,0:T(1,128)S(1)} reshape(f32[384]{0:T(512)} %param.12) | data formatting | bytes 3072 | tf_op jit(solution)/shard_map/reshape | solution.py:316
  2.0 0.7 %reshape.15.pbias = f32[1,384]{1,0:T(1,128)S(1)} reshape(f32[384]{0:T(512)} %param.15) | data formatting | bytes 3072 | tf_op jit(solution)/shard_map/reshape | solution.py:316
  2.7 0.0 copy-start
  2.7 1.2 %copy-done = bf16[384,1152]{1,0:T(8,128)(2,1)S(1)} copy-done((bf16[384,1152]{1,0:T(8,128)(2,1)S(1)}, bf16[384,1152]{1,0:T(8,128)(2,1)}, u32[]{:S(2)}) %copy-start) | copy-done | bytes 884760
  3.9 0.0 copy-start.1
  3.9 1.0 %copy-done.1 = bf16[384,384]{1,0:T(8,128)(2,1)S(1)} copy-done((bf16[384,384]{1,0:T(8,128)(2,1)S(1)}, bf16[384,384]{1,0:T(8,128)(2,1)}, u32[]{:S(2)}) %copy-start.1) | copy-done | bytes 294936
  4.9 0.0 copy-start.2
  4.9 0.9 %copy-done.2 = bf16[1,2,120,384]{3,2,1,0:T(8,128)(2,1)S(1)} copy-done((bf16[1,2,120,384]{3,2,1,0:T(8,128)(2,1)S(1)}, bf16[1,2,120,384]{3,2,1,0:T(8,128)(2,1)}, u32[]{:S(2)}) %copy-start.2) | copy-done | bytes 184344
  5.8 38.5 %shard_map.82 = f32[1,2,120,384]{3,2,1,0:T(8,128)S(1)} custom-call(bf16[1,2,120,384]{3,2,1,0:T(8,128)(2,1)S(1)} %copy-done.2, f32[1,384]{1,0:T(1,128)S(1)} %reshape.12.cgain, bf16[3,3,3,384,384]{4,3,2,1,0:T(8,128)(2,1)} %cw_hbm.1, f32[1,384]{1,0:T(1,128)S(1)} %reshape.13.cbias, f32[1,384]{1,0:T(1,128)S(1)} %reshape.14.again, bf16[384,1152]{1,0:T(8,128)(2,1)S(1)} %copy-done, ...), custom_call_target="tpu_custom_call" | custom-call | tf_op jit(solution)/shard_map/pallas_call | solution.py:289
  44.3 0.7 %copy.10 = f32[1,2,120,384]{3,2,1,0:T(8,128)} copy(f32[1,2,120,384]{3,2,1,0:T(8,128)S(1)} %shard_map.82) | data formatting | bytes 737280
Async XLA Ops:
  2.7 1.2 %copy-start = (bf16[384,1152]{1,0:T(8,128)(2,1)S(1)}, bf16[384,1152]{1,0:T(8,128)(2,1)}, u32[]{:S(2)}) copy-start(bf16[384,1152]{1,0:T(8,128)(2,1)} %qkv_hbm.1) | copy-start | bytes 2654212
  3.9 1.0 %copy-start.1 = (bf16[384,384]{1,0:T(8,128)(2,1)S(1)}, bf16[384,384]{1,0:T(8,128)(2,1)}, u32[]{:S(2)}) copy-start(bf16[384,384]{1,0:T(8,128)(2,1)} %proj_hbm.1) | copy-start | bytes 884740
  4.9 0.9 %copy-start.2 = (bf16[1,2,120,384]{3,2,1,0:T(8,128)(2,1)S(1)}, bf16[1,2,120,384]{3,2,1,0:T(8,128)(2,1)}, u32[]{:S(2)}) copy-start(bf16[1,2,120,384]{3,2,1,0:T(8,128)(2,1)} %lat_hbm.1) | copy-start | bytes 552964

commit v2 on v1

v2 whole, which is shorter than its diff:
```python
import functools

import jax
import jax.numpy as jnp
from jax import lax
from jax.experimental import pallas as pl
from jax.experimental.pallas import tpu as pltpu
from jax.sharding import PartitionSpec as P

MESH = pl.DeviceIdType.MESH
F32, BF16 = jnp.float32, jnp.bfloat16
MATE_DIRECT, FAR_DIRECT = False, False
CHUNKS, CROSS_FIRST = (5, 3, 2), 1


def normed(v, gain):
    return v * lax.rsqrt(jnp.mean(v * v, axis=-1, keepdims=True) + 1e-06) * gain


def dot(a, b):
    return jnp.dot(a, b, preferred_element_type=F32)


def kernel(
    count, frames, padded, chunks,
    lat_hbm, cgain_hbm, cw_hbm, cbias_hbm, again_hbm, qkv_hbm, proj_hbm, pbias_hbm, out,
    lat, cgain, cbias, again, pbias, cw, qkv, proj, frame, taps, block, gathered, query, high, denom, accum,
    in_sem, vec_sem, cw_sem, later_send, later_recv, send, recv, up1, dn1, up2, dn2, to_a, line_sem, b_sem, a_sem,
):
    t, s = lax.axis_index("tm"), lax.axis_index("space")
    rows, cols, chans = lat.shape[1:]
    cells = rows * cols
    size = cells // chunks
    na = chunks - CROSS_FIRST
    early = chunks
    hi, lo = lax.div(s, 2), lax.rem(s, 2)
    nhi = count // 2
    mate = s + 1 - 2 * lo
    twin = t + 1 - 2 * lax.rem(t, 2)
    old = t >= 2
    near = [
        (s >= 1, {"space": s - 1}),
        (s < count - 1, {"space": s + 1}),
        (s >= 2, {"space": s - 2}),
        (s < count - 2, {"space": s + 2}),
        (t >= 2, {"tm": t - 2}),
        (t < frames - 2, {"tm": t + 2}),
        (True, {"tm": twin}),
    ]
    barrier = pltpu.get_barrier_semaphore()
    for there, device in near:
        @pl.when(there)
        def _():
            pl.semaphore_signal(barrier, inc=1, device_id=device, device_id_type=MESH)

    get_lat = pltpu.make_async_copy(lat_hbm, lat, in_sem.at[0])
    get_qkv = pltpu.make_async_copy(qkv_hbm, qkv, in_sem.at[1])
    get_proj = pltpu.make_async_copy(proj_hbm, proj, in_sem.at[2])
    get_cw = [pltpu.make_async_copy(cw_hbm.at[i], cw.at[i], cw_sem.at[i]) for i in range(3)]
    pairs = [(cgain_hbm, cgain), (cbias_hbm, cbias), (again_hbm, again), (pbias_hbm, pbias)]
    get_vec = [pltpu.make_async_copy(a, b, vec_sem.at[i]) for i, (a, b) in enumerate(pairs)]
    get_lat.start()
    for copy in get_vec:
        copy.start()
    for i in (2, 0, 1):
        get_cw[i].start()
    get_qkv.start()
    get_proj.start()

    def zero_row(f, r):
        frame[f, r] = jnp.zeros((padded, chans), BF16)

    @pl.when(s == 0)
    def _():
        zero_row(2, 0)
        zero_row(0, 0)

    @pl.when(s == count - 1)
    def _():
        zero_row(2, rows + 1)
        zero_row(0, rows + 1)

    get_lat.wait()
    get_vec[0].wait()
    for r in range(rows):
        act = jax.nn.silu(normed(lat[0, r].astype(F32), cgain[...][None]))
        act = jnp.concatenate([act, jnp.zeros((padded - cols, chans), F32)], axis=0)
        frame[2, r + 1] = act.astype(BF16)

    pl.semaphore_wait(barrier, sum(there.astype(jnp.int32) for there, _ in near[:-1]) + 1)

    def remote(src, dst, ssem, rsem, device):
        return pltpu.make_async_remote_copy(
            src_ref=src, dst_ref=dst, send_sem=ssem, recv_sem=rsem,
            device_id=device, device_id_type=MESH,
        )

    far = s - 1 + 2 * lo
    far_here = jnp.logical_and(far >= 0, far < count)
    mate_src, mate_dst = jnp.where(lo == 0, rows, 1), jnp.where(lo == 0, 0, rows + 1)
    far_src, far_dst = jnp.where(lo == 0, 1, rows), jnp.where(lo == 0, rows + 1, 0)
    mate_land, far_land = rows + 1 - mate_dst, rows + 1 - far_dst
    onward = t < frames - 2

    later = [
        remote(frame.at[2, r], frame.at[0, r], later_send.at[r - 1], later_recv.at[r - 1], {"tm": t + 2})
        for r in range(1, rows + 1)
    ]

    def edge(src, f, to_mate, k, device):
        at, to = (mate_src, mate_dst) if to_mate else (far_src, far_dst)
        return remote(frame.at[src, at], frame.at[f, to], send.at[k], recv.at[k], device)

    def landing(f, of_mate, k):
        ref = frame.at[f, mate_land if of_mate else far_land]
        return remote(ref, ref, send.at[k], recv.at[k], {"space": mate})

    own_mate = edge(2, 2, True, 0, {"space": mate})
    own_far = edge(2, 2, False, 1, {"space": far})
    if MATE_DIRECT:
        old_mate, gives_mate = edge(2, 0, True, 2, {"space": mate, "tm": t + 2}), onward
    else:
        old_mate, gives_mate = edge(0, 0, True, 2, {"space": mate}), old
    if FAR_DIRECT:
        old_far, gives_far = edge(2, 0, False, 3, {"space": far, "tm": t + 2}), jnp.logical_and(far_here, onward)
    else:
        old_far, gives_far = edge(0, 0, False, 3, {"space": far}), jnp.logical_and(far_here, old)
    twin_own = remote(frame.at[2], frame.at[1], send.at[4], recv.at[4], {"tm": twin})
    twin_old = remote(frame.at[0], frame.at[1], send.at[4], recv.at[4], {"tm": twin})
    is_even = lax.rem(t, 2) == 0
    gives_old = jnp.logical_and(t >= 3, jnp.logical_not(is_even))

    pl.when(far_here)(own_far.start)
    own_mate.start()

    @pl.when(onward)
    def _():
        for copy in later:
            copy.start()

    if FAR_DIRECT:
        pl.when(gives_far)(old_far.start)
    if MATE_DIRECT:
        pl.when(gives_mate)(old_mate.start)

    @pl.when(old)
    def _():
        for copy in later:
            copy.wait_recv()
        if not FAR_DIRECT:
            pl.when(far_here)(old_far.start)
        if not MATE_DIRECT:
            old_mate.start()

    landing(2, True, 0).wait_recv()
    pl.when(far_here)(landing(2, False, 1).wait_recv)
    pl.when(is_even)(twin_own.start)

    def conv_step(i, first):
        left = jnp.concatenate(
            [frame[i, pl.ds(j, rows)].reshape(rows * padded, chans) for j in range(3)], axis=1
        )
        for k in range(3):
            right = jnp.concatenate([cw[i, j, k] for j in range(3)], axis=0)
            part = dot(left, right)
            taps[k] = part if first else taps[k] + part

    get_cw[2].wait()
    conv_step(2, True)
    get_cw[0].wait()

    @pl.when(old)
    def _():
        landing(0, True, 2).wait_recv()
        pl.when(far_here)(landing(0, False, 3).wait_recv)
        pl.when(gives_old)(twin_old.start)
        conv_step(0, False)

    get_cw[1].wait()

    @pl.when(t >= 1)
    def _():
        twin_own.wait_recv()
        conv_step(1, False)

    for copy in get_vec[1:]:
        copy.wait()
    for r in range(rows):
        at = pl.ds(r * padded, padded)
        sums = pltpu.roll(taps[0, at], 1, 0) + taps[1, at] + pltpu.roll(taps[2, at], padded - 1, 0)
        sums = sums[:cols] + cbias[...][None]
        block[pl.ds(r * cols, cols)] = lat[0, r].astype(F32) + sums
    attn_in = normed(block[...], again[...][None]).astype(BF16)
    gathered[s] = attn_in

    def part(h, lane, c):
        return gathered.at[2 * h + lane, pl.ds(c * size, size)]

    def along(h, c, step):
        sems = up1 if step > 0 else dn1
        ref = part(h, lo, c)
        return remote(ref, ref, sems.at[h, c], line_sem.at[h, c], {"space": s + 2 * step})

    def along_b(h, c, step):
        sems = up2 if step > 0 else dn2
        ref = part(h, 1 - lo, c)
        return remote(ref, ref, sems.at[h, c - na], b_sem.at[h, c - na], {"space": s + 2 * step})

    def over(h, c, mine=True):
        ref = part(h, lo if mine else 1 - lo, c)
        return remote(ref, ref, to_a.at[h, c], a_sem.at[h, c], {"space": mate})

    above, below = hi < nhi - 1, hi > 0
    for c in range(na, chunks):
        over(hi, c).start()
    for c in range(chunks):
        pl.when(above)(along(hi, c, 1).start)
        pl.when(below)(along(hi, c, -1).start)
        if c < na:
            over(hi, c).start()

    get_qkv.wait()
    get_proj.wait()
    query[...] = dot(attn_in, qkv[:, :chans]).astype(BF16)
    high[...] = jnp.full(high.shape, -jnp.inf, F32)
    denom[...] = jnp.zeros(denom.shape, F32)
    accum[...] = jnp.zeros(accum.shape, F32)

    for c in range(na, chunks):
        over(hi, c, False).wait_recv()
        pl.when(above)(along_b(hi, c, 1).start)
        pl.when(below)(along_b(hi, c, -1).start)

    def attend(h):
        feats = gathered[pl.ds(2 * h, 2)].reshape(2 * cells, chans)
        keys = dot(feats, qkv[:, chans : 2 * chans]).astype(BF16)
        values = dot(feats, qkv[:, 2 * chans :]).astype(BF16)
        scores = lax.dot_general(
            query[...], keys, (((1,), (1,)), ((), ())), preferred_element_type=F32
        ) * (chans ** -0.5)
        top = jnp.maximum(high[...], jnp.max(scores, axis=-1, keepdims=True))
        factor = jnp.exp(high[...] - top)
        weights = jnp.exp(scores - top)
        high[...] = top
        denom[...] = denom[...] * factor + jnp.sum(weights, axis=-1, keepdims=True)
        accum[...] = accum[...] * factor + dot(weights.astype(BF16), values)

    def arrive(h, c, here, onward, direction):
        @pl.when(here)
        def _():
            along(h, c, direction).wait_recv()
            pl.when(onward)(along(h, c, direction).start)
            if c < na:
                over(h, c).start()

    def arrive_b(h, c, here, onward, direction):
        @pl.when(here)
        def _():
            along_b(h, c, direction).wait_recv()
            pl.when(onward)(along_b(h, c, direction).start)

    def finish(h, here):
        @pl.when(here)
        def _():
            for c in range(na):
                over(h, c, False).wait_recv()
            attend(h)

    def finish_own():
        for c in range(na):
            over(hi, c, False).wait_recv()
        attend(hi)

    def arrivals(d, some):
        for c in some:
            arrive(hi - d, c, hi - d >= 0, above, 1)
            arrive(hi + d, c, hi + d < nhi, below, -1)

    def step(d, carry):
        arrivals(d, range(early))
        for c in range(na, chunks):
            arrive_b(hi - d, c, hi - d >= 0, above, 1)
            arrive_b(hi + d, c, hi + d < nhi, below, -1)

        @pl.when(d == 1)
        def _():
            finish_own()

        @pl.when(d > 1)
        def _():
            finish(hi - d + 1, hi - d + 1 >= 0)
            finish(hi + d - 1, hi + d - 1 < nhi)

        arrivals(d, range(early, chunks))
        return carry

    lax.fori_loop(1, nhi, step, 0)
    finish(hi - nhi + 1, hi - nhi + 1 >= 0)
    finish(hi + nhi - 1, hi + nhi - 1 < nhi)

    mixed = (accum[...] / denom[...]).astype(BF16)
    decoded = block[...] + (dot(mixed, proj[...]) + pbias[...][None])
    for r in range(rows):
        out[0, r] = decoded[r * cols : (r + 1) * cols]

    @pl.when(onward)
    def _():
        for copy in later:
            copy.wait_send()

    own_mate.wait_send()
    pl.when(far_here)(own_far.wait_send)
    pl.when(gives_mate)(old_mate.wait_send)
    pl.when(gives_far)(old_far.wait_send)
    pl.when(is_even)(twin_own.wait_send)
    pl.when(gives_old)(twin_old.wait_send)

    def drain(h, carry):
        for c in range(na):
            over(h, c).wait_send()

        @pl.when(jnp.logical_and(h <= hi, above))
        def _():
            for c in range(chunks):
                along(h, c, 1).wait_send()
            for c in range(na, chunks):
                along_b(h, c, 1).wait_send()

        @pl.when(jnp.logical_and(h >= hi, below))
        def _():
            for c in range(chunks):
                along(h, c, -1).wait_send()
            for c in range(na, chunks):
                along_b(h, c, -1).wait_send()

        return carry

    lax.fori_loop(0, nhi, drain, 0)
    for c in range(na, chunks):
        over(hi, c).wait_send()


def solution(mesh):
    count, frames = mesh.shape["space"], mesh.shape["tm"]

    def on_device(
        latents, conv_gain, conv_weight, conv_bias, attn_gain, qkv_weight, proj_weight, proj_bias
    ):
        _, rows, cols, chans = latents.shape
        padded = (cols + 16) // 16 * 16
        cells = rows * cols
        nhi = count // 2
        chunks = next(n for n in CHUNKS if cells % (16 * n) == 0)
        anywhere = pl.BlockSpec(memory_space=pltpu.HBM)
        local = pl.BlockSpec(memory_space=pltpu.VMEM)
        dma = pltpu.SemaphoreType.DMA
        return pl.pallas_call(
            functools.partial(kernel, count, frames, padded, chunks),
            out_shape=jax.ShapeDtypeStruct(latents.shape, F32),
            in_specs=[anywhere] * 8,
            out_specs=local,
            scratch_shapes=[
                pltpu.VMEM(latents.shape, BF16),
                *[pltpu.VMEM((chans,), F32)] * 4,
                pltpu.VMEM(conv_weight.shape, BF16),
                pltpu.VMEM(qkv_weight.shape, BF16),
                pltpu.VMEM(proj_weight.shape, BF16),
                pltpu.VMEM((3, rows + 2, padded, chans), BF16),
                pltpu.VMEM((3, rows * padded, chans), F32),
                pltpu.VMEM((cells, chans), F32),
                pltpu.VMEM((count, cells, chans), BF16),
                pltpu.VMEM((cells, chans), BF16),
                pltpu.VMEM((cells, 1), F32),
                pltpu.VMEM((cells, 1), F32),
                pltpu.VMEM((cells, chans), F32),
                dma((3,)), dma((4,)), dma((3,)), dma((rows,)), dma((rows,)), dma((5,)), dma((5,)),
                dma((nhi, chunks)), dma((nhi, chunks)), dma((nhi, CROSS_FIRST)), dma((nhi, CROSS_FIRST)),
                dma((nhi, chunks)), dma((nhi, chunks)), dma((nhi, CROSS_FIRST)), dma((nhi, chunks)),
            ],
            compiler_params=pltpu.CompilerParams(
                collective_id=0, has_side_effects=True, vmem_limit_bytes=60 * 2**20
            ),
        )(
            latents, conv_gain, conv_weight, conv_bias,
            attn_gain, qkv_weight, proj_weight, proj_bias,
        )

    in_specs = (P("tm", "space", None, None), P(), P(), P(), P(), P(), P(), P())
    return jax.shard_map(
        on_device, mesh=mesh, in_specs=in_specs,
        out_specs=P("tm", "space", None, None), check_vma=False,
    )
```

time: 45.3 us -> 37.7 us (0.83)
  local copies, waits for them, and re-layouts: 6.52 us -> 1.75 us
  Pallas kernels: 38.5 us -> 35.3 us
    pallas_call x1, Pallas kernels: 38.5 us -> 35.3 us  [on_device(): pl.pallas_call(functools.partial(kernel, count, frames, padded, chunks),...]
    reshape x4 -> x0, local copies, waits for them, and re-layouts: 2.73 us -> none  [the longest x1 0.68 us: on_device(): conv_bias.reshape(1, chans)]
    unnamed x7 -> x1, local copies, waits for them, and re-layouts: 3.79 us -> 1.75 us
where the time goes in v2:
time: 37.7 us; the launch traced here: 37.1 us
  Pallas kernels  35.3 us (94%)
  local copies, waits for them, and re-layouts  1.75 us (5%)
    pallas_call x1, Pallas kernels, on_device(): pl.pallas_call(functools.partial(kernel, count, frames, padded, chunks),...  35.3 us
    unnamed x1, local copies, waits for them, and re-layouts  1.75 us

profile of v2, /device:TPU:4, one launch (start us, length us, event | category | flops | bytes accessed | tf_op | source)
XLA Modules:
  0.0 37.1 jit_solution(9188773816081979295)
XLA Ops:
  0.0 35.3 %shard_map.82 = f32[1,2,120,384]{3,2,1,0:T(8,128)} custom-call(bf16[1,2,120,384]{3,2,1,0:T(8,128)(2,1)} %lat_hbm.1, f32[384]{0:T(512)} %cgain_hbm.1, bf16[3,3,3,384,384]{4,3,2,1,0:T(8,128)(2,1)} %cw_hbm.1, f32[384]{0:T(512)} %cbias_hbm.1, f32[384]{0:T(512)} %again_hbm.1, bf16[384,1152]{1,0:T(8,128)(2,1)} %qkv_hbm.1, bf16[384,384]{1,0:T(8,128)(2,1)} %proj_hbm.1, ...), custom_call_target="tpu_custom_call" | custom-call | tf_op jit(solution)/shard_map/pallas_call | solution.py:357
  35.3 1.7 %copy.10 = f32[1,2,120,384]{3,2,1,0:T(8,128)} copy(f32[1,2,120,384]{3,2,1,0:T(8,128)} %shard_map.82) | data formatting | bytes 737280
